TPU v7x, 32 devices: a whole 2x2x4 slice. The times are simulated.
32 devices in a mesh: row: 8 (over y, x, core), col: 4 (over z).
Axes of the slice: x: 2, y: 2, z: 4, core: 2. Of those that a mesh axis runs over, the one named last changes fastest.
Arguments:
- reduced_basis: bfloat16 [5, 96, 16384], P(None, None, ('row', 'col')), may hold values from -6 to 6
- cell_jacobian: float32 [5, 5, 16384], P(None, None, ('row', 'col')), may hold values from -4 to 4
- face_cells: int32 [2, 32768], P(None, ('row', 'col')), may hold values from 0 to 511, as said below
- face_jacobian: float32 [2, 5, 5, 32768], P(None, None, None, ('row', 'col')), may hold values from -3 to 3
- limiter_flags: int32 [32768], P(('row', 'col')), may hold values 0 or 1
- viscosity: float32 [5], replicated, may hold values from 0.1 to 1
- ghost_cells: int32 [5120], P(('row', 'col')), may hold values from 0 to 511
- ghost_jacobian: float32 [5, 5, 5120], P(None, None, ('row', 'col')), may hold values from -3 to 3
- ghost_counts: int32 [256], P(('row', 'col')), may hold values from 4 to 32, as said below
- receive_cells: int32 [5120], P(('row', 'col')), may hold values from 0 to 511
- coordinates: float32 [96], replicated, may hold values from -5 to 5
- base_residual: float32 [5, 16384], P(None, ('row', 'col')), may hold values from -6 to 6
Outputs:
- test_basis: bfloat16 [5, 96, 16384], P(None, None, ('row', 'col'))
- triangular_factor: float32 [97, 97], replicated
- gauss_step: float32 [96], replicated
Inputs may be any that keep to these rules, and one draw needn't show every extreme that they name: `face_cells`: the two cells of a face differ and lie at most 64 apart modulo 512. `ghost_counts`: entry 8 p + m counts the used slots of block m of partition p: from half of the block's size to all of it (32 for the first four blocks, 8 for the last four); in every draw some partition uses all slots of all its blocks.
All inputs are finite; a program needn't handle non-finite values. No bound on the sum of `limiter_flags` on one device may be relied on, other than what follows from the above.
Results may differ from a plain program's by a relative error of at most 0.0095.
Values may be sent and summed in bfloat16 or wider, within the bound.
A program may use at most 64 MiB of HBM per device.

v0:
```python
import jax
import jax.numpy as jnp
import numpy as np
from jax import lax
from jax.sharding import PartitionSpec as P

FACE_CAP = 32
EDGE_CAP = 8


direction_offsets = ((-1, 0), (1, 0), (0, -1), (0, 1), (-1, -1), (-1, 1), (1, -1), (1, 1))


def extended(block, sides, width):
    for axis, dim in sides:
        count = lax.axis_size(axis)
        forward = [(i, i + 1) for i in range(count - 1)]
        backward = [(target, source) for source, target in forward]
        low = lax.ppermute(
            lax.slice_in_dim(block, block.shape[dim] - width, None, axis=dim), axis, forward
        )
        high = lax.ppermute(lax.slice_in_dim(block, 0, width, axis=dim), axis, backward)
        block = jnp.concatenate([low, block, high], axis=dim)
    return block


def block_sizes():
    return [FACE_CAP] * 4 + [EDGE_CAP] * 4


def slot_limits(counts):
    capacity_each = block_sizes()
    slot_owner = np.concatenate(
        [
            np.full(total_quantity, position, np.int32)
            for position, total_quantity in enumerate(capacity_each)
        ]
    )
    slot_position = np.concatenate(
        [np.arange(total_quantity, dtype=np.int32) for total_quantity in capacity_each]
    )
    compare = slot_owner[None, :] == np.arange(8, dtype=np.int32)[:, None]
    slot_limit = jnp.sum(jnp.where(compare, counts[:, None], 0), axis=0)
    return slot_position < slot_limit


def upper_cholesky(matrix):
    order = matrix.shape[0]
    indices = jnp.arange(order, dtype=jnp.int32)

    def column_step(column, lower):
        row_vector = lax.dynamic_slice_in_dim(lower, column, 1, 0)[0]
        target = lax.dynamic_slice_in_dim(matrix, column, 1, 1)[:, 0]
        remain = target - jnp.dot(lower, row_vector, precision=lax.Precision.HIGHEST)
        pivot = jnp.sqrt(jnp.sum(jnp.where(indices == column, remain, 0.0)))
        new_column = jnp.where(
            indices > column, remain / pivot, jnp.where(indices == column, pivot, 0.0)
        )
        return lax.dynamic_update_slice_in_dim(lower, new_column[:, None], column, 1)

    lower = lax.fori_loop(0, order, column_step, jnp.zeros_like(matrix))
    return lower.T


def upper_solve(upper, rhs):
    order = upper.shape[0]
    indices = jnp.arange(order, dtype=jnp.int32)

    def row_step(turn, solution):
        place = order - 1 - turn
        upper_row = lax.dynamic_slice_in_dim(upper, place, 1, 0)[0]
        known = jnp.dot(upper_row, solution, precision=lax.Precision.HIGHEST)
        pivot = jnp.sum(jnp.where(indices == place, upper_row, 0.0))
        target = jnp.sum(jnp.where(indices == place, rhs, 0.0))
        return jnp.where(indices == place, (target - known) / pivot, solution)

    return lax.fori_loop(0, order, row_step, jnp.zeros_like(rhs))


def local(
    reduced_basis,
    cell_jacobian,
    face_cells,
    face_jacobian,
    limiter_flags,
    viscosity,
    ghost_cells,
    ghost_jacobian,
    ghost_counts,
    receive_cells,
    coordinates,
    base_residual,
):
    fields, mode_count, cell_count = reduced_basis.shape
    face_count = face_cells.shape[1]
    devices = lax.axis_size("row") * lax.axis_size("col")
    row_scale = (fields * cell_count * devices) ** (-0.5)
    gathered = jnp.take(reduced_basis, ghost_cells, axis=2)
    partial_value = jnp.einsum(
        "gfs,fks->gks",
        ghost_jacobian,
        gathered,
        precision=lax.Precision.HIGHEST,
        preferred_element_type=jnp.float32,
    )
    slot_kept = slot_limits(ghost_counts)
    partial_value = jnp.where(slot_kept[None, None, :], partial_value, 0.0).astype(jnp.bfloat16)
    blocks = []
    slot_start = 0
    for block_width in block_sizes():
        blocks.append(partial_value[:, :, slot_start : slot_start + block_width])
        slot_start += block_width
    zero_block = jnp.zeros((fields, mode_count, FACE_CAP), jnp.bfloat16)
    layout = [[zero_block, zero_block, zero_block] for position in range(3)]
    for direction, offset_pair in enumerate(direction_offsets):
        row_offset, col_offset = offset_pair
        widened = jnp.pad(
            blocks[direction], ((0, 0), (0, 0), (0, FACE_CAP - blocks[direction].shape[2]))
        )
        layout[1 + row_offset][1 + col_offset] = widened
    buffer = jnp.stack([jnp.stack(layout_row) for layout_row in layout])
    padded = extended(buffer, (("row", 0), ("col", 1)), 1)
    arrived = []
    for direction, offset_pair in enumerate(direction_offsets):
        row_offset, col_offset = offset_pair
        arrived.append(
            padded[2 - 2 * row_offset, 2 - 2 * col_offset][:, :, : blocks[direction].shape[2]]
        )
    incoming_block = jnp.concatenate(arrived, axis=2)
    jacobian_projection = jnp.einsum(
        "irx,rtx->itx",
        cell_jacobian,
        reduced_basis,
        precision=lax.Precision.HIGHEST,
        preferred_element_type=jnp.float32,
    )
    face_width = face_count // 4

    def face_step(block_index, image_sum):
        face_start = block_index * face_width
        face_pair = lax.dynamic_slice_in_dim(face_cells, face_start, face_width, 1)
        block_jacobian = lax.dynamic_slice_in_dim(face_jacobian, face_start, face_width, 3)
        flag_block = lax.dynamic_slice_in_dim(limiter_flags, face_start, face_width, 0)
        left_basis = jnp.take(reduced_basis, face_pair[0], axis=2)
        right_basis = jnp.take(reduced_basis, face_pair[1], axis=2)
        damping = viscosity[:, None, None] * flag_block.astype(jnp.float32)[None, None, :]
        difference = left_basis.astype(jnp.float32) - right_basis.astype(jnp.float32)
        to_left = (
            jnp.einsum(
                "gfn,fkn->gkn",
                block_jacobian[0],
                right_basis,
                precision=lax.Precision.HIGHEST,
                preferred_element_type=jnp.float32,
            )
            + damping * difference
        )
        to_right = (
            jnp.einsum(
                "gfn,fkn->gkn",
                block_jacobian[1],
                left_basis,
                precision=lax.Precision.HIGHEST,
                preferred_element_type=jnp.float32,
            )
            - damping * difference
        )
        image_sum = image_sum.at[:, :, face_pair[0]].add(to_left)
        return image_sum.at[:, :, face_pair[1]].add(to_right)

    jacobian_projection = lax.fori_loop(0, 4, face_step, jacobian_projection)
    jacobian_projection = jacobian_projection.at[:, :, receive_cells].add(
        incoming_block.astype(jnp.float32)
    )
    test_basis = jacobian_projection.astype(jnp.bfloat16)
    residual_vector = base_residual + row_scale * jnp.einsum(
        "fkc,k->fc",
        test_basis,
        coordinates,
        precision=lax.Precision.HIGHEST,
        preferred_element_type=jnp.float32,
    )
    stacked = jnp.concatenate(
        [test_basis, residual_vector.astype(jnp.bfloat16)[:, None, :]], axis=1
    )
    gram_matrix = lax.dot_general(
        stacked, stacked, (((0, 2), (0, 2)), ((), ())), preferred_element_type=jnp.float32
    ) * (row_scale * row_scale)
    gram_sum = lax.psum(gram_matrix, ("row", "col"))
    upper_factor = upper_cholesky(gram_sum)
    solved = upper_solve(
        upper_factor[:mode_count, :mode_count], upper_factor[:mode_count, mode_count]
    )
    gauss_step = -solved / row_scale
    return (test_basis, upper_factor, gauss_step)


def solution(mesh):
    placed = (
        P(None, None, ("row", "col")),
        P(None, None, ("row", "col")),
        P(None, ("row", "col")),
        P(None, None, None, ("row", "col")),
        P(("row", "col")),
        P(),
        P(("row", "col")),
        P(None, None, ("row", "col")),
        P(("row", "col")),
        P(("row", "col")),
        P(),
        P(None, ("row", "col")),
    )
    return jax.shard_map(
        local,
        mesh=mesh,
        in_specs=placed,
        out_specs=(P(None, None, ("row", "col")), P(), P()),
        check_vma=False,
    )
```

profile of v0, /device:TPU:0, one launch (start us, length us, event | category | flops | bytes accessed | tf_op | source)
XLA Modules:
  0.0 665.1 jit_solution(16717988866778029805)
XLA Ops:
  2.1 2.7 copy.38
  4.8 1.1 copy.43
  6.0 1.9 gather_fusion.2
  8.0 1.4 fusion.26
  10.9 1.3 collective-permute-start
  13.0 3.7 collective-permute-start.1
  16.7 2.0 copy.39
  18.7 3.8 convolution_bitcast_fusion.3
  22.6 140.8 %while.44 = (s32[]{:T(128)}, f32[5,96,512]{1,0,2:T(8,128)S(1)}, s32[2,1024]{1,0:T(2,128)}, bf16[5,96,512]{1,0,2:T(8,128)(2,1)}, f32[2,5,5,1024]{3,0,2,1:T(2,128)...) while((s32[]{:T(128)}, f32[5,96,512]{1,0,2:T(8,128)S(1)}, ...), condition=%wide.region_3.5_spmd, body=%wide.region_0.4_spmd.sunk | while | flops 16967176 | bytes 6201055 | solution.py:171
  22.6 0.8 compare_select_fusion.11
  23.4 1.0 constant_dynamic-slice_fusion.6
  24.4 1.3 copy.60
  26.7 2.8 gather_fusion
  29.5 2.8 gather_fusion.1
  32.3 3.8 fusion.69
  36.1 8.3 %scatter_fusion = f32[5,96,512]{1,0,2:T(8,128)S(1)} fusion(f32[5,96,512]{1,0,2:T(8,128)S(1)} %get-tuple-element.605, s32[256]{0:T(256)S(1)} %bitcast.190, f32[256,5,96]{2,1,0:T(8,128)S(1)} %fusion.69), kind=kCustom, calls=%fused_computation.3.clone.1 | custom fusion | flops 122880 | bytes 1475584 | tf_op jit(solution)/shard_map/while/body/eval_jaxpr/scatter-add | solution.py:168
  44.4 1.3 copy.61
  45.8 3.7 fusion.70
  49.5 8.3 %scatter_fusion.1 = f32[5,96,512]{1,0,2:T(8,128)S(1)} fusion(f32[5,96,512]{1,0,2:T(8,128)S(1)} %scatter_fusion, s32[256]{0:T(256)S(1)} %bitcast.189, f32[256,5,96]{2,1,0:T(8,128)S(1)} %fusion.70), kind=kCustom, calls=%fused_computation.4.clone.1 | custom fusion | flops 122880 | bytes 1475584 | tf_op jit(solution)/shard_map/while/body/eval_jaxpr/scatter-add | solution.py:169
  57.8 0.8 compare_select_fusion.11
  58.6 1.0 constant_dynamic-slice_fusion.6
  59.6 1.3 copy.60
  61.8 2.8 gather_fusion
  64.7 2.8 gather_fusion.1
  67.5 3.8 fusion.69
  71.3 8.3 %scatter_fusion = f32[5,96,512]{1,0,2:T(8,128)S(1)} fusion(f32[5,96,512]{1,0,2:T(8,128)S(1)} %get-tuple-element.605, s32[256]{0:T(256)S(1)} %bitcast.190, f32[256,5,96]{2,1,0:T(8,128)S(1)} %fusion.69), kind=kCustom, calls=%fused_computation.3.clone.1 | custom fusion | flops 122880 | bytes 1475584 | tf_op jit(solution)/shard_map/while/body/eval_jaxpr/scatter-add | solution.py:168
  79.6 1.3 copy.61
  81.0 3.7 fusion.70
  84.6 8.3 %scatter_fusion.1 = f32[5,96,512]{1,0,2:T(8,128)S(1)} fusion(f32[5,96,512]{1,0,2:T(8,128)S(1)} %scatter_fusion, s32[256]{0:T(256)S(1)} %bitcast.189, f32[256,5,96]{2,1,0:T(8,128)S(1)} %fusion.70), kind=kCustom, calls=%fused_computation.4.clone.1 | custom fusion | flops 122880 | bytes 1475584 | tf_op jit(solution)/shard_map/while/body/eval_jaxpr/scatter-add | solution.py:169
  93.0 0.8 compare_select_fusion.11
  93.8 1.0 constant_dynamic-slice_fusion.6
  94.8 1.3 copy.60
  97.0 2.8 gather_fusion
  99.9 2.8 gather_fusion.1
  102.7 3.8 fusion.69
  106.5 8.3 %scatter_fusion = f32[5,96,512]{1,0,2:T(8,128)S(1)} fusion(f32[5,96,512]{1,0,2:T(8,128)S(1)} %get-tuple-element.605, s32[256]{0:T(256)S(1)} %bitcast.190, f32[256,5,96]{2,1,0:T(8,128)S(1)} %fusion.69), kind=kCustom, calls=%fused_computation.3.clone.1 | custom fusion | flops 122880 | bytes 1475584 | tf_op jit(solution)/shard_map/while/body/eval_jaxpr/scatter-add | solution.py:168
  114.8 1.3 copy.61
  116.1 3.7 fusion.70
  119.8 8.3 %scatter_fusion.1 = f32[5,96,512]{1,0,2:T(8,128)S(1)} fusion(f32[5,96,512]{1,0,2:T(8,128)S(1)} %scatter_fusion, s32[256]{0:T(256)S(1)} %bitcast.189, f32[256,5,96]{2,1,0:T(8,128)S(1)} %fusion.70), kind=kCustom, calls=%fused_computation.4.clone.1 | custom fusion | flops 122880 | bytes 1475584 | tf_op jit(solution)/shard_map/while/body/eval_jaxpr/scatter-add | solution.py:169
  128.1 0.8 compare_select_fusion.11
  129.0 1.0 constant_dynamic-slice_fusion.6
  130.0 1.3 copy.60
  132.2 2.8 gather_fusion
  135.1 2.8 gather_fusion.1
  137.9 3.8 fusion.69
  141.7 8.3 %scatter_fusion = f32[5,96,512]{1,0,2:T(8,128)S(1)} fusion(f32[5,96,512]{1,0,2:T(8,128)S(1)} %get-tuple-element.605, s32[256]{0:T(256)S(1)} %bitcast.190, f32[256,5,96]{2,1,0:T(8,128)S(1)} %fusion.69), kind=kCustom, calls=%fused_computation.3.clone.1 | custom fusion | flops 122880 | bytes 1475584 | tf_op jit(solution)/shard_map/while/body/eval_jaxpr/scatter-add | solution.py:168
  150.0 1.3 copy.61
  151.3 3.7 fusion.70
  155.0 8.3 %scatter_fusion.1 = f32[5,96,512]{1,0,2:T(8,128)S(1)} fusion(f32[5,96,512]{1,0,2:T(8,128)S(1)} %scatter_fusion, s32[256]{0:T(256)S(1)} %bitcast.189, f32[256,5,96]{2,1,0:T(8,128)S(1)} %fusion.70), kind=kCustom, calls=%fused_computation.4.clone.1 | custom fusion | flops 122880 | bytes 1475584 | tf_op jit(solution)/shard_map/while/body/eval_jaxpr/scatter-add | solution.py:169
  163.4 1.0 constant_dynamic-update-slice_fusion.3
  164.4 0.9 constant_dynamic-update-slice_fusion.2
  165.3 1.0 fusion.34
  166.3 0.9 constant_dynamic-update-slice_fusion.1
  167.3 1.0 constant_dynamic-update-slice_fusion
  168.4 1.3 collective-permute-start.2
  169.7 5.6 collective-permute-start.3
  175.3 0.9 fusion.39
  176.1 0.9 fusion.38
  177.0 4.8 collective-permute-done.2
  181.8 1.1 collective-permute-done.3
  183.1 6.0 scatter_fusion.2
  190.3 40.9 %psum.7 = f32[97,97]{1,0:T(8,128)S(1)} all-reduce(f32[97,97]{1,0:T(8,128)S(1)} %fusion.27), channel_id=1, replica_groups=mesh['row'=8,'col'=4] {'row','col'}, use_global_device_ids=true, to_apply=%region_6.8 | all-reduce | flops 9409 | bytes 75272 | tf_op jit(solution)/shard_map/psum | solution.py:189
  231.3 190.3 %while.45 = (s32[]{:T(128)}, f32[97,97]{1,0:T(8,128)S(1)}, f32[97,97]{0,1:T(8,128)S(1)}, s32[]{:T(128)}, s32[]{:T(128)}) while((s32[]{:T(128)}, f32[97,97]{1,0:T(8,128)S(1)}, f32[97,97]{0,1:T(8,128)S(1)}, s32[]{:T(128)}, s32[]{:T(128)}) %tuple.139), condition=%wide.region_9.11_spmd.clone.clone, body=%wide.region_7.10_spmd.clone.clone.sunk | while | flops 113782 | bytes 58617 | solution.py:61
  422.0 242.6 %while.46 = (s32[]{:T(128)}, f32[96]{0:T(128)S(1)}, f32[96]{0:T(128)S(1)}, f32[96,96]{1,0:T(8,128)S(1)}, s32[]{:T(128)}, /*index=5*/s32[]{:T(128)}, s32[]{:T(128)}, s32[]{:T(128)}) while((s32[]{:T(128)}, f32[96]{0:T(128)S(1)}, f32[96]{0:T(128)S(1)}, f32[96,96]{1,0:T(8,128)S(1)}, s32[]{:T(128)}, /*index=5*/s32[]{:T(128)}, ...), condition=%wide.region_13.15_spmd.clone, body=%wide.region_10.14_spmd.clone.sunk | while | flops 1062 | bytes 2122 | solution.py:77
  (667 shorter events, 190.5 us)
Async XLA Ops:
  0.6 189.0 %copy-start = (f32[96]{0:T(128)S(1)}, f32[96]{0:T(128)}, u32[]{:S(2)}) copy-start(f32[96]{0:T(128)} %param.32) | copy-start | bytes 1156
  0.6 7.3 %copy-start.9 = (pred[8,160]{1,0:T(8,128)(4,1)S(1)}, pred[8,160]{1,0:T(8,128)(4,1)}, u32[]{:S(2)}) copy-start(pred[8,160]{1,0:T(8,128)(4,1)} %constant.161.clone) | copy-start | bytes 3844
  0.7 7.3 %copy-start.11 = (s32[160]{0:T(256)S(1)}, s32[160]{0:T(256)}, u32[]{:S(2)}) copy-start(s32[160]{0:T(256)} %constant.162.clone) | copy-start | bytes 1924
  0.7 7.2 %copy-start.12 = (s32[8]{0:T(128)S(1)}, s32[8]{0:T(128)}, u32[]{:S(2)}) copy-start(s32[8]{0:T(128)} %param.30) | copy-start | bytes 100
  4.8 11.9 %copy-start.6 = (f32[5,5,512]{2,1,0:T(8,128)S(1)}, f32[5,5,512]{2,1,0:T(8,128)}, u32[]{:S(2)}) copy-start(f32[5,5,512]{2,1,0:T(8,128)} %param.23) | copy-start | bytes 153604
  10.2 2.0 copy-start.4
  10.2 6.5 copy-start.3
  10.9 156.3 %collective-permute-start = (bf16[1,3,5,96,32]{3,2,4,1,0:T(8,128)(2,1)}, bf16[1,3,5,96,32]{3,2,4,1,0:T(8,128)(2,1)}, u32[]{:S(2)}, u32[]{:S(2)}) collective-permute-start(bf16[1,3,5,96,32]{3,2,4,1,0:T(8,128)(2,1)} %maximum_bitcast_fusion), channel_id=1, source_target_pairs={{4,0},{8,4},{12,8},{16,12},{20,16},{24,20},{28,24},{5,1},{9,5},{13... | collective-permute-start | bytes 276488 | tf_op jit(solution)/shard_map/ppermute | solution.py:22
  12.2 4.5 copy-start.2
  13.0 150.5 %collective-permute-start.1 = (bf16[1,3,5,96,32]{3,2,4,1,0:T(8,128)(2,1)}, bf16[1,3,5,96,32]{3,2,4,1,0:T(8,128)(2,1)}, u32[]{:S(2)}, u32[]{:S(2)}) collective-permute-start(bf16[1,3,5,96,32]{3,2,4,1,0:T(8,128)(2,1)} %maximum_bitcast_fusion.1), channel_id=1, source_target_pairs={{0,4},{4,8},{8,12},{12,16},{16,20},{20,24},{24,28},{1,5},{5,9},{9,... | collective-permute-start | bytes 276488 | tf_op jit(solution)/shard_map/ppermute | solution.py:19
  18.7 3.8 copy-start.8
  22.6 140.8 %copy-start.10 = (s32[160]{0:T(256)S(1)}, s32[160]{0:T(256)}, u32[]{:S(2)}) copy-start(s32[160]{0:T(256)} %param.31) | copy-start | bytes 1924
  168.4 13.4 %collective-permute-start.2 = (bf16[5,1,5,96,32]{3,2,4,1,0:T(8,128)(2,1)S(1)}, bf16[5,1,5,96,32]{3,2,4,1,0:T(8,128)(2,1)S(1)}, u32[]{:S(2)}, u32[]{:S(2)}) collective-permute-start(bf16[5,1,5,96,32]{3,2,4,1,0:T(8,128)(2,1)S(1)} %get-tuple-element.458), channel_id=1, source_target_pairs={{1,0},{2,1},{3,2},{5,4},{6,5},{7,6},{9,8},{10,9},{11,10},{13,12},{... | collective-permute-start | bytes 460808 | tf_op jit(solution)/shard_map/ppermute | solution.py:22
  169.7 13.3 %collective-permute-start.3 = (bf16[5,1,5,96,32]{3,2,4,1,0:T(8,128)(2,1)S(1)}, bf16[5,1,5,96,32]{3,2,4,1,0:T(8,128)(2,1)S(1)}, u32[]{:S(2)}, u32[]{:S(2)}) collective-permute-start(bf16[5,1,5,96,32]{3,2,4,1,0:T(8,128)(2,1)S(1)} %get-tuple-element.457), channel_id=1, source_target_pairs={{0,1},{1,2},{2,3},{4,5},{5,6},{6,7},{8,9},{9,10},{10,11},{12,13},{... | collective-permute-start | bytes 460808 | tf_op jit(solution)/shard_map/ppermute | solution.py:19
  183.1 6.8 %copy-start.7 = (f32[5,512]{1,0:T(8,128)S(1)}, f32[5,512]{1,0:T(8,128)}, u32[]{:S(2)}) copy-start(f32[5,512]{1,0:T(8,128)} %param.33) | copy-start | bytes 30724
  189.6 475.4 %copy-start.1 = (bf16[5,96,512]{2,1,0:T(8,128)(2,1)}, bf16[5,96,512]{2,1,0:T(8,128)(2,1)S(1)}, u32[]{:S(2)}) copy-start(bf16[5,96,512]{2,1,0:T(8,128)(2,1)S(1)} %copy.44) | copy-start | bytes 1474564
  421.8 243.3 %copy-start.5 = (f32[97,97]{0,1:T(8,128)}, f32[97,97]{0,1:T(8,128)S(1)}, u32[]{:S(2)}) copy-start(f32[97,97]{0,1:T(8,128)S(1)} %copy.47) | copy-start | bytes 112912
where the time goes:
time: 673 us; the launch traced here: 665 us
  loops' own time  252 us (37%)
  other arithmetic  147 us (22%)
  matrix products  114 us (17%)
  local copies, waits for them, and re-layouts  92.2 us (14%)
  blocking collectives  40.9 us (6%)
  starting transfers between devices  11.9 us (2%)
    another operation x1, loops' own time, upper_solve(): return lax.fori_loop(0, order, row_step, jnp.zeros_like(rhs))  182 us
    dot_general x97, matrix products, column_step(): jnp.dot(lower, row_vector, precision=lax.Precision.HIGHEST)  77.9 us
    another operation x1, loops' own time, upper_cholesky(): lower = lax.fori_loop(0, order, column_step, jnp.zeros_like(matrix))  70.2 us
    reduce_sum x96, other arithmetic, row_step(): pivot = jnp.sum(jnp.where(indices == place, upper_row, 0.0))  59.6 us
    psum x1, blocking collectives, local(): gram_sum = lax.psum(gram_matrix, ('row', 'col'))  40.9 us
    scatter-add x4, other arithmetic, face_step(): image_sum = image_sum.at[:, :, face_pair[0]].add(to_left)  33.2 us
    scatter-add x4, other arithmetic, face_step(): return image_sum.at[:, :, face_pair[1]].add(to_right)  33.2 us
    dynamic_update_slice x97, local copies, waits for them, and re-layouts, column_step(): lax.dynamic_update_slice_in_dim(lower, new_column[:, None], column, 1)  30.1 us
  transfers between devices with their start and end apart: 4, of which 2 were waited for; matrix products, arithmetic and copies ran while one was open for 23% of the time, Pallas kernels for 0%

commit v1 on v0

v1 whole, which is shorter than its diff:
```python
import functools

import jax
import jax.numpy as jnp
from jax import lax
from jax.experimental import pallas as pl
from jax.experimental.pallas import tpu as pltpu
from jax.sharding import PartitionSpec as P

FACE_CAP = 32
EDGE_CAP = 8
EDGE_ROWS = 16
OFFSETS = ((-1, 0), (1, 0), (0, -1), (0, 1), (-1, -1), (-1, 1), (1, -1), (1, 1))
SLOTS = 4 * FACE_CAP + 4 * EDGE_CAP
SENT_ROWS = 4 * FACE_CAP + 4 * EDGE_ROWS
MESH = pl.DeviceIdType.MESH
BF16 = jnp.bfloat16
F32 = jnp.float32


def block_rows(m):
    if m < 4:
        return m * FACE_CAP, FACE_CAP
    return 4 * FACE_CAP + (m - 4) * EDGE_ROWS, EDGE_ROWS


def one_hot(cells, count):
    rows = lax.broadcasted_iota(jnp.int32, (count, cells.shape[1]), 0)
    return jnp.where(rows == cells, 1.0, 0.0).astype(BF16)


def matmul(a, b, dims):
    return lax.dot_general(a, b, (dims, ((), ())), preferred_element_type=F32)


def assemble(
    nrow, ncol, row_scale, tiles, chunk,
    basis, cellj, facec, facej, flags, visc, ghostc, ghostj, counts, recvc, coords, base,
    tb_out, gram_out,
    hot, terms, left_s, right_s, sent, got, stacked, gram_s, parts, mine, summed,
    halo_send, halo_recv, up_send, up_recv, down_send, down_recv,
):
    fields, modes, cells = basis.shape
    wide = fields * modes
    faces = facec.shape[1]
    devices = nrow * ncol
    row, col = lax.axis_index("row"), lax.axis_index("col")
    me = row * ncol + col

    def place(d):
        return (lax.div(d, jnp.int32(ncol)), lax.rem(d, jnp.int32(ncol)))

    barrier = pltpu.get_barrier_semaphore()

    @pl.loop(0, devices)
    def _(d):
        @pl.when(d != me)
        def _():
            pl.semaphore_signal(barrier, inc=1, device_id=place(d), device_id_type=MESH)

    flat = basis[...].reshape(wide, cells)

    slot = lax.broadcasted_iota(jnp.int32, (1, SLOTS), 1)
    limit = jnp.zeros((1, SLOTS), jnp.int32)
    start = 0
    for m in range(8):
        width = FACE_CAP if m < 4 else EDGE_CAP
        inside = (slot >= start) & (slot < start + width)
        limit = jnp.where(inside, counts[m] + start, limit)
        start += width
    kept = slot < limit
    ghosts = matmul(flat, one_hot(ghostc[...], cells), ((1,), (0,)))
    pieces = []
    for g in range(fields):
        total = None
        for f in range(fields):
            entry = jnp.where(kept, ghostj[g, f : f + 1, :], 0.0)
            term = entry * ghosts[f * modes : (f + 1) * modes]
            total = term if total is None else total + term
        pieces.append(total.astype(BF16))
    partial = jnp.concatenate(pieces, axis=0)
    lane = lax.broadcasted_iota(jnp.int32, (SENT_ROWS, SLOTS), 1)
    sub = lax.broadcasted_iota(jnp.int32, (SENT_ROWS, SLOTS), 0)
    edge = lane - 4 * FACE_CAP
    target = jnp.where(edge < 0, lane, lane + (edge >> 3) * (EDGE_ROWS - EDGE_CAP))
    spread = jnp.where(sub == target, 1.0, 0.0).astype(BF16)
    sent[...] = matmul(spread, partial, ((1,), (1,))).astype(BF16)
    placed = matmul(spread, one_hot(recvc[...], cells), ((1,), (1,))).astype(BF16)

    def inside_grid(dr, dc):
        ok = (row + dr >= 0) & (row + dr < nrow)
        return ok & (col + dc >= 0) & (col + dc < ncol)

    for m, (dr, dc) in enumerate(OFFSETS):
        first, count = block_rows(m)

        @pl.when(jnp.logical_not(inside_grid(-dr, -dc)))
        def _():
            got[first : first + count, :] = jnp.zeros((count, wide), BF16)

    pl.semaphore_wait(barrier, devices - 1)

    def halo(m):
        dr, dc = OFFSETS[m]
        first, count = block_rows(m)
        return pltpu.make_async_remote_copy(
            src_ref=sent.at[pl.ds(first, count)],
            dst_ref=got.at[pl.ds(first, count)],
            send_sem=halo_send.at[m],
            recv_sem=halo_recv.at[m],
            device_id=(row + dr, col + dc),
            device_id_type=MESH,
        )

    for m, (dr, dc) in enumerate(OFFSETS):
        @pl.when(inside_grid(dr, dc))
        def _():
            halo(m).start()

    @pl.loop(0, faces // chunk)
    def _(step):
        at = pl.multiple_of(step * chunk, chunk)
        span = pl.ds(at, chunk)
        span_b = pl.ds(pl.multiple_of(at + faces, chunk), chunk)
        pair = facec[:, span]
        hot_a = one_hot(pair[0:1], cells)
        hot_b = one_hot(pair[1:2], cells)
        hot[:, span] = hot_a
        hot[:, span_b] = hot_b
        left_s[...] = matmul(flat, hot_a, ((1,), (0,)))
        right_s[...] = matmul(flat, hot_b, ((1,), (0,)))
        flag = flags[:, span].astype(F32)
        mark = jnp.where(
            lax.broadcasted_iota(jnp.int32, (16, chunk), 0) == 0, flag, 0.0
        ).astype(BF16)
        for side, values, where_to in ((0, right_s, span), (1, left_s, span_b)):
            jac = facej[side, :, :, span]
            for g in range(fields):
                total = None
                for f in range(fields):
                    entry = jac[g, f : f + 1, :]
                    if f == g:
                        entry = entry - visc[g] * flag
                    term = entry * values[f * modes : (f + 1) * modes, :]
                    total = term if total is None else total + term
                terms[g * modes : (g + 1) * modes, where_to] = total.astype(BF16)
            terms[wide : wide + 16, where_to] = mark

    image = matmul(terms[...], hot[...], ((1,), (1,)))
    flagged = image[wide : wide + 1, :]
    rows = []
    for g in range(fields):
        total = image[g * modes : (g + 1) * modes, :]
        for f in range(fields):
            entry = cellj[g, f : f + 1, :]
            if f == g:
                entry = entry + visc[g] * flagged
            total = total + entry * basis[f].astype(F32)
        rows.append(total)

    for m, (dr, dc) in enumerate(OFFSETS):
        @pl.when(inside_grid(-dr, -dc))
        def _():
            halo(m).wait_recv()

    arrived = matmul(got[...], placed, ((0,), (0,)))
    c = coords[...]
    high = c.astype(BF16).astype(F32)
    mid = (c - high).astype(BF16).astype(F32)
    low = c - high - mid
    sub16 = lax.broadcasted_iota(jnp.int32, (16, modes), 0)
    weights = jnp.where(
        sub16 == 0, high, jnp.where(sub16 == 1, mid, jnp.where(sub16 == 2, low, 0.0))
    ).astype(BF16)
    top = lax.broadcasted_iota(jnp.int32, (16, cells), 0) == 0
    gram = None
    for g in range(fields):
        basis_g = (rows[g] + arrived[g * modes : (g + 1) * modes]).astype(BF16)
        tb_out[g] = basis_g
        stacked[g, :modes, :] = basis_g
        shift = jnp.sum(matmul(weights, basis_g, ((1,), (0,))), axis=0, keepdims=True)
        resid = base[g : g + 1, :] + row_scale * shift
        stacked[g, modes : modes + 16, :] = jnp.where(top, resid, 0.0).astype(BF16)
        stacked[g, modes + 16 :, :] = jnp.zeros((128 - modes - 16, cells), BF16)
        x = stacked[g]
        part = matmul(x, x, ((1,), (1,)))
        gram = part if gram is None else gram + part
    gram_s[...] = gram[: tiles * 8].reshape(tiles, 8, 128)

    def owner(t):
        return (t * devices) // tiles

    my_tile = lax.div(me * tiles + (devices - 1), jnp.int32(devices))
    tile = jnp.minimum(my_tile, tiles - 1)
    owns = (my_tile < tiles) & (lax.div(tile * devices, jnp.int32(tiles)) == me)

    def up(t):
        o = owner(t)
        return pltpu.make_async_remote_copy(
            src_ref=gram_s.at[t],
            dst_ref=parts.at[me],
            send_sem=up_send.at[t],
            recv_sem=up_recv.at[me],
            device_id=(jnp.int32(o // ncol), jnp.int32(o % ncol)),
            device_id_type=MESH,
        )

    for t in range(tiles):
        @pl.when(me != owner(t))
        def _():
            up(t).start()

        @pl.when(me == owner(t))
        def _():
            parts[me] = gram_s[t]

    def down(d):
        return pltpu.make_async_remote_copy(
            src_ref=mine,
            dst_ref=summed.at[tile],
            send_sem=down_send.at[d],
            recv_sem=down_recv.at[tile],
            device_id=place(d),
            device_id_type=MESH,
        )

    @pl.when(owns)
    def _():
        @pl.loop(0, devices)
        def _(d):
            @pl.when(d != me)
            def _():
                pltpu.make_async_remote_copy(
                    src_ref=mine,
                    dst_ref=parts.at[d],
                    send_sem=down_send.at[d],
                    recv_sem=up_recv.at[d],
                    device_id=place(d),
                    device_id_type=MESH,
                ).wait_recv()

        total = jnp.sum(parts[...], axis=0)
        mine[...] = total
        summed[tile] = total

        @pl.loop(0, devices)
        def _(d):
            @pl.when(d != me)
            def _():
                down(d).start()

    for t in range(tiles):
        @pl.when(me != owner(t))
        def _():
            pltpu.make_async_remote_copy(
                src_ref=mine,
                dst_ref=summed.at[t],
                send_sem=up_send.at[t],
                recv_sem=down_recv.at[t],
                device_id=place(jnp.int32(owner(t))),
                device_id_type=MESH,
            ).wait_recv()

    gram_out[...] = summed[...]

    for m, (dr, dc) in enumerate(OFFSETS):
        @pl.when(inside_grid(dr, dc))
        def _():
            halo(m).wait_send()

    for t in range(tiles):
        @pl.when(me != owner(t))
        def _():
            up(t).wait_send()

    @pl.when(owns)
    def _():
        @pl.loop(0, devices)
        def _(d):
            @pl.when(d != me)
            def _():
                down(d).wait_send()


def factor(modes, row_scale, gram, tb_in, upper, step, tb_out, sem):
    passing = pltpu.make_async_copy(tb_in, tb_out, sem)
    passing.start()
    tiles = gram.shape[0]
    order = modes + 1
    shape = (8, 128)
    sub = lax.broadcasted_iota(jnp.int32, shape, 0)
    lane = lax.broadcasted_iota(jnp.int32, shape, 1)

    def across(x, s):
        return jnp.broadcast_to(x[s : s + 1, :], shape)

    rows = [gram[t] * (row_scale * row_scale) for t in range(tiles)]
    done = [jnp.zeros(shape, F32) for _ in range(tiles)]
    for p in range(tiles):
        columns = range(8 * p, min(8 * p + 8, order))
        held = {
            j: [jnp.broadcast_to(rows[t][:, j : j + 1], shape) for t in range(tiles)]
            for j in columns
        }
        for j in columns:
            s = j % 8
            here = sub == s
            inverse = lax.rsqrt(across(held[j][p], s))
            pivot_row = across(rows[p], s) * inverse
            done[p] = jnp.where(here, pivot_row, done[p])
            if j == modes:
                break
            scaled = [x * inverse for x in held[j]]
            for t in range(tiles):
                new = rows[t] - scaled[t] * pivot_row
                rows[t] = jnp.where(here, pivot_row * inverse, new) if t == p else new
            for i in columns:
                if i <= j:
                    continue
                entry = across(scaled[p], i % 8)
                for t in range(tiles):
                    new = held[i][t] - scaled[t] * entry
                    held[i][t] = jnp.where(here, entry * inverse, new) if t == p else new
    solved = jnp.zeros(shape, F32)
    for t in range(tiles):
        kept = jnp.where(lane >= sub + 8 * t, done[t], 0.0)
        count = min(8, order - 8 * t)
        upper[8 * t : 8 * t + count, :] = kept[:count, :order]
        if 8 * t < modes:
            last = jnp.broadcast_to(rows[t][:, modes : modes + 1], shape)
            solved = solved + jnp.where(lane == sub + 8 * t, last, 0.0)
    step[...] = (jnp.sum(solved, axis=0, keepdims=True) * (-1.0 / row_scale))[:, :modes]
    passing.wait()


def local(
    nrow, ncol,
    reduced_basis, cell_jacobian, face_cells, face_jacobian, limiter_flags, viscosity,
    ghost_cells, ghost_jacobian, ghost_counts, receive_cells, coordinates, base_residual,
):
    fields, modes, cells = reduced_basis.shape
    faces = face_cells.shape[1]
    devices = nrow * ncol
    wide = fields * modes
    row_scale = float((fields * cells * devices) ** (-0.5))
    tiles = (modes + 1 + 7) // 8
    chunk = 256
    vmem = pl.BlockSpec(memory_space=pltpu.VMEM)
    smem = pl.BlockSpec(memory_space=pltpu.SMEM)
    dma = pltpu.SemaphoreType.DMA
    test_basis, gram = pl.pallas_call(
        functools.partial(assemble, nrow, ncol, row_scale, tiles, chunk),
        out_shape=(
            jax.ShapeDtypeStruct((fields, modes, cells), BF16),
            jax.ShapeDtypeStruct((tiles, 8, 128), F32),
        ),
        in_specs=[vmem, vmem, vmem, vmem, vmem, smem, vmem, vmem, smem, vmem, vmem, vmem],
        out_specs=(vmem, vmem),
        scratch_shapes=[
            pltpu.VMEM((cells, 2 * faces), BF16),
            pltpu.VMEM((wide + 16, 2 * faces), BF16),
            pltpu.VMEM((wide, chunk), F32),
            pltpu.VMEM((wide, chunk), F32),
            pltpu.VMEM((SENT_ROWS, wide), BF16),
            pltpu.VMEM((SENT_ROWS, wide), BF16),
            pltpu.VMEM((fields, 128, cells), BF16),
            pltpu.VMEM((tiles, 8, 128), F32),
            pltpu.VMEM((devices, 8, 128), F32),
            pltpu.VMEM((8, 128), F32),
            pltpu.VMEM((tiles, 8, 128), F32),
            dma((8,)), dma((8,)), dma((tiles,)), dma((devices,)), dma((devices,)), dma((tiles,)),
        ],
        compiler_params=pltpu.CompilerParams(
            collective_id=0, has_side_effects=True, vmem_limit_bytes=48 * 1024 * 1024
        ),
        cost_estimate=pl.CostEstimate(
            flops=8 * wide * cells * faces, bytes_accessed=3_000_000, transcendentals=0
        ),
        name="assemble",
    )(
        reduced_basis, cell_jacobian, face_cells, face_jacobian, limiter_flags.reshape(1, -1),
        viscosity, ghost_cells.reshape(1, -1), ghost_jacobian, ghost_counts,
        receive_cells.reshape(1, -1), coordinates.reshape(1, -1), base_residual,
    )
    upper, step, test_basis = pl.pallas_call(
        functools.partial(factor, modes, row_scale),
        out_shape=(
            jax.ShapeDtypeStruct((modes + 1, modes + 1), F32),
            jax.ShapeDtypeStruct((1, modes), F32),
            jax.ShapeDtypeStruct((fields, modes, cells), BF16),
        ),
        in_specs=[vmem, pl.BlockSpec(memory_space=pl.ANY)],
        out_specs=(vmem, vmem, pl.BlockSpec(memory_space=pl.ANY)),
        scratch_shapes=[pltpu.SemaphoreType.DMA],
        name="factor",
    )(gram, test_basis)
    return test_basis, upper, step.reshape(modes)


def solution(mesh):
    both = ("row", "col")
    placed = (
        P(None, None, both), P(None, None, both), P(None, both), P(None, None, None, both),
        P(both), P(), P(both), P(None, None, both), P(both), P(both), P(), P(None, both),
    )
    return jax.shard_map(
        functools.partial(local, mesh.shape["row"], mesh.shape["col"]),
        mesh=mesh,
        in_specs=placed,
        out_specs=(P(None, None, both), P(), P()),
        check_vma=False,
    )
```

time: 673 us -> 47.3 us (0.07); the launches traced: 665 us -> 46.9 us
  loops' own time: 252 us -> 0 us
  other arithmetic: 147 us -> 0 us
  matrix products: 114 us -> 0 us
  local copies, waits for them, and re-layouts: 92.2 us -> 4.78 us
  Pallas kernels: 0 us -> 41.4 us
  blocking collectives: 40.9 us -> 0 us
  starting transfers between devices: 11.9 us -> 0 us
    another operation x3 -> x0, loops' own time: 252 us -> none  [the longest x1 182 us: upper_solve(): return lax.fori_loop(0, order, row_step, jnp.zeros_like(rhs))]
    dot_general x109 -> x0, matrix products: 114 us -> none  [the longest x97 77.9 us: column_step(): jnp.dot(lower, row_vector, precision=lax.Precision.HIGHEST)]
    scatter-add x9 -> x0, other arithmetic: 72.3 us -> none  [the longest x4 33.2 us: face_step(): image_sum = image_sum.at[:, :, face_pair[0]].add(to_left)]
    reduce_sum x97 -> x0, other arithmetic: 59.7 us -> none  [the longest x96 59.6 us: row_step(): pivot = jnp.sum(jnp.where(indices == place, upper_row, 0.0))]
    pallas_call x0 -> x2, Pallas kernels: none -> 41.4 us  [the longest x1 23.9 us: local(): pl.pallas_call(functools.partial(assemble, nrow, ncol, row_scale, tiles,...]
    psum x1 -> x0, blocking collectives: 40.9 us -> none  [local(): gram_sum = lax.psum(gram_matrix, ('row', 'col'))]
    dynamic_update_slice x97 -> x0, local copies, waits for them, and re-layouts: 30.1 us -> none  [column_step(): lax.dynamic_update_slice_in_dim(lower, new_column[:, None], column, 1)]
    gather x9 -> x0, local copies, waits for them, and re-layouts: 24.5 us -> none  [the longest x4 11.3 us: face_step(): right_basis = jnp.take(reduced_basis, face_pair[1], axis=2)]
  transfers between devices with their start and end apart: 4 -> 0, of which waited for: 2 -> 0; matrix products, arithmetic and copies ran while one was open for 23% -> 0% of each run, Pallas kernels for 0% -> 0%
where the time goes in v1:
time: 47.3 us; the launch traced here: 46.9 us
  Pallas kernels  41.4 us (88%)
  local copies, waits for them, and re-layouts  4.78 us (10%)
  between operations  0.79 us (2%)
    pallas_call x1, Pallas kernels, local(): pl.pallas_call(functools.partial(assemble, nrow, ncol, row_scale, tiles,...  23.9 us
    pallas_call x1, Pallas kernels, local(): pl.pallas_call(functools.partial(factor, modes, row_scale), out_shape=(ja...  17.4 us
    unnamed x27, local copies, waits for them, and re-layouts  4.78 us

profile of v1, /device:TPU:0, one launch (start us, length us, event | category | flops | bytes accessed | tf_op | source)
XLA Modules:
  0.0 46.9 jit_solution(11876843471113755528)
XLA Ops:
  0.6 0.0 copy-start.2
  0.6 0.0 copy-start.4
  0.7 0.0 copy-start.7
  0.7 0.0 copy-start.8
  0.7 0.0 copy-start.9
  0.7 0.0 copy-start.10
  0.7 0.0 copy-start.11
  0.7 0.0 copy-start.12
  0.7 1.1 %copy.15.facej = f32[2,5,5,1024]{3,2,1,0:T(8,128)S(1)} copy(f32[2,5,5,1024]{3,0,2,1:T(2,128)} %param.15) | data formatting | bytes 409600 | tf_op args[3]
  1.8 0.0 copy-done.2
  1.8 0.0 copy-done.4
  1.8 0.0 copy-done.7
  1.8 0.0 copy-done.8
  1.8 0.0 copy-done.9
  1.8 0.0 copy-done.10
  1.8 0.0 copy-done.11
  1.8 0.0 copy-done.12
  1.9 0.0 copy-start.3
  1.9 0.9 %copy-done.3 = f32[5,5,512]{2,1,0:T(8,128)S(1)} copy-done((f32[5,5,512]{2,1,0:T(8,128)S(1)}, f32[5,5,512]{2,1,0:T(8,128)}, u32[]{:S(2)}) %copy-start.3) | copy-done | bytes 51224
  2.7 0.0 copy-start.5
  2.7 0.7 %copy-done.5 = f32[5,512]{1,0:T(8,128)S(1)} copy-done((f32[5,512]{1,0:T(8,128)S(1)}, f32[5,512]{1,0:T(8,128)}, u32[]{:S(2)}) %copy-start.5) | copy-done | bytes 10264
  3.5 0.0 copy-start.6
  3.5 0.7 %copy-done.6 = s32[2,1024]{1,0:T(2,128)S(1)} copy-done((s32[2,1024]{1,0:T(2,128)S(1)}, s32[2,1024]{1,0:T(2,128)}, u32[]{:S(2)}) %copy-start.6) | copy-done | bytes 8216
  4.2 23.9 %assemble.1 = (bf16[5,96,512]{2,1,0:T(8,128)(2,1)S(1)}, f32[13,8,128]{2,1,0:T(8,128)S(1)}) custom-call(bf16[5,96,512]{2,1,0:T(8,128)(2,1)S(1)} %copy-done.2, f32[5,5,512]{2,1,0:T(8,128)S(1)} %copy-done.3, s32[2,1024]{1,0:T(2,128)S(1)} %copy-done.6, f32[2,5,5,1024]{3,2,1,0:T(8,128)S(1)} %copy.15.facej, s32[1,1024]{1,0:T(1,128)S(1)} %bitcast.5, ...), custom_call_target="tpu_custom_call" | custom-call | flops 2013265920 | bytes 3000000 | tf_op jit(solution)/shard_map/assemble/pallas_call | solution.py:351
  28.1 0.0 copy-start
  28.1 0.8 %copy-done = bf16[5,96,512]{2,1,0:T(8,128)(2,1)} copy-done((bf16[5,96,512]{2,1,0:T(8,128)(2,1)}, bf16[5,96,512]{2,1,0:T(8,128)(2,1)S(1)}, u32[]{:S(2)}) %copy-start) | copy-done | bytes 491544
  28.9 0.0 copy-start.1
  28.9 0.6 %copy-done.1 = f32[13,8,128]{2,1,0:T(8,128)} copy-done((f32[13,8,128]{2,1,0:T(8,128)}, f32[13,8,128]{2,1,0:T(8,128)S(1)}, u32[]{:S(2)}) %copy-start.1) | copy-done | bytes 53272
  29.5 17.4 %factor.1 = (f32[97,97]{1,0:T(8,128)}, f32[1,96]{1,0:T(1,128)}, bf16[5,96,512]{2,1,0:T(8,128)(2,1)}) custom-call(f32[13,8,128]{2,1,0:T(8,128)} %copy-done.1, bf16[5,96,512]{2,1,0:T(8,128)(2,1)} %copy-done), custom_call_target="tpu_custom_call" | custom-call | tf_op jit(solution)/shard_map/factor/pallas_call | solution.py:385
Async XLA Ops:
  0.6 1.1 %copy-start.2 = (bf16[5,96,512]{2,1,0:T(8,128)(2,1)S(1)}, bf16[5,96,512]{2,1,0:T(8,128)(2,1)}, u32[]{:S(2)}) copy-start(bf16[5,96,512]{2,1,0:T(8,128)(2,1)} %basis.1) | copy-start | bytes 1474564
  0.6 1.1 %copy-start.4 = (f32[5,5,160]{2,1,0:T(8,128)S(1)}, f32[5,5,160]{2,1,0:T(8,128)}, u32[]{:S(2)}) copy-start(f32[5,5,160]{2,1,0:T(8,128)} %ghostj.1) | copy-start | bytes 48004
  0.7 1.1 %copy-start.7 = (s32[1024]{0:T(1024)S(1)}, s32[1024]{0:T(1024)}, u32[]{:S(2)}) copy-start(s32[1024]{0:T(1024)} %param.16) | copy-start | bytes 12292
  0.7 1.1 %copy-start.8 = (s32[160]{0:T(256)S(1)}, s32[160]{0:T(256)}, u32[]{:S(2)}) copy-start(s32[160]{0:T(256)} %param.18) | copy-start | bytes 1924
  0.7 1.1 %copy-start.9 = (s32[160]{0:T(256)S(1)}, s32[160]{0:T(256)}, u32[]{:S(2)}) copy-start(s32[160]{0:T(256)} %param.21) | copy-start | bytes 1924
  0.7 1.1 %copy-start.10 = (f32[5]{0:T(128)S(1)}, f32[5]{0:T(128)}, u32[]{:S(2)}) copy-start(f32[5]{0:T(128)} %visc.1) | copy-start | bytes 64
  0.7 1.1 %copy-start.11 = (s32[8]{0:T(128)S(1)}, s32[8]{0:T(128)}, u32[]{:S(2)}) copy-start(s32[8]{0:T(128)} %counts.1) | copy-start | bytes 100
  0.7 1.1 %copy-start.12 = (f32[96]{0:T(128)S(1)}, f32[96]{0:T(128)}, u32[]{:S(2)}) copy-start(f32[96]{0:T(128)} %param.22) | copy-start | bytes 1156
  1.9 0.9 %copy-start.3 = (f32[5,5,512]{2,1,0:T(8,128)S(1)}, f32[5,5,512]{2,1,0:T(8,128)}, u32[]{:S(2)}) copy-start(f32[5,5,512]{2,1,0:T(8,128)} %cellj.1) | copy-start | bytes 153604
  2.7 0.7 %copy-start.5 = (f32[5,512]{1,0:T(8,128)S(1)}, f32[5,512]{1,0:T(8,128)}, u32[]{:S(2)}) copy-start(f32[5,512]{1,0:T(8,128)} %base.1) | copy-start | bytes 30724
  3.5 0.7 %copy-start.6 = (s32[2,1024]{1,0:T(2,128)S(1)}, s32[2,1024]{1,0:T(2,128)}, u32[]{:S(2)}) copy-start(s32[2,1024]{1,0:T(2,128)} %facec.1) | copy-start | bytes 24580
  28.1 0.8 %copy-start = (bf16[5,96,512]{2,1,0:T(8,128)(2,1)}, bf16[5,96,512]{2,1,0:T(8,128)(2,1)S(1)}, u32[]{:S(2)}) copy-start(bf16[5,96,512]{2,1,0:T(8,128)(2,1)S(1)} %get-tuple-element.9.tb_in) | copy-start | bytes 1474564
  28.9 0.6 %copy-start.1 = (f32[13,8,128]{2,1,0:T(8,128)}, f32[13,8,128]{2,1,0:T(8,128)S(1)}, u32[]{:S(2)}) copy-start(f32[13,8,128]{2,1,0:T(8,128)S(1)} %get-tuple-element.8.gram) | copy-start | bytes 159748

commit v2 on v1

--- a/solution.py
+++ b/solution.py
@@ -35,9 +35,11 @@
 
 def assemble(
     nrow, ncol, row_scale, tiles, chunk,
-    basis, cellj, facec, facej, flags, visc, ghostc, ghostj, counts, recvc, coords, base,
+    basis_h, cellj_h, facec_h, facej_h, flags_h, visc_h, ghostc_h, ghostj_h, counts_h, recvc_h,
+    coords_h, base_h,
     tb_out, gram_out,
-    hot, terms, left_s, right_s, sent, got, stacked, gram_s, parts, mine, summed,
+    basis, cellj, facec, facej, flags, visc, ghostc, ghostj, counts, recvc, coords, base, in_sem,
+    tb_sem, hot, terms, left_s, right_s, sent, got, stacked, gram_s, parts, mine, summed,
     halo_send, halo_recv, up_send, up_recv, down_send, down_recv,
 ):
     fields, modes, cells = basis.shape
@@ -50,6 +52,21 @@
     def place(d):
         return (lax.div(d, jnp.int32(ncol)), lax.rem(d, jnp.int32(ncol)))
 
+    names = ("basis", "ghostc", "counts", "ghostj", "recvc", "facec", "flags", "visc", "facej",
+             "cellj", "coords", "base")
+    inputs = dict(
+        basis=(basis_h, basis), ghostc=(ghostc_h, ghostc), counts=(counts_h, counts),
+        ghostj=(ghostj_h, ghostj), recvc=(recvc_h, recvc), facec=(facec_h, facec),
+        flags=(flags_h, flags), visc=(visc_h, visc), facej=(facej_h, facej),
+        cellj=(cellj_h, cellj), coords=(coords_h, coords), base=(base_h, base),
+    )
+
+    def fetch(name):
+        return pltpu.make_async_copy(*inputs[name], in_sem.at[names.index(name)])
+
+    for name in names:
+        fetch(name).start()
+
     barrier = pltpu.get_barrier_semaphore()
 
     @pl.loop(0, devices)
@@ -58,6 +75,8 @@
         def _():
             pl.semaphore_signal(barrier, inc=1, device_id=place(d), device_id_type=MESH)
 
+    for name in names[:5]:
+        fetch(name).wait()
     flat = basis[...].reshape(wide, cells)
 
     slot = lax.broadcasted_iota(jnp.int32, (1, SLOTS), 1)
@@ -117,6 +136,9 @@
         def _():
             halo(m).start()
 
+    for name in names[5:9]:
+        fetch(name).wait()
+
     @pl.loop(0, faces // chunk)
     def _(step):
         at = pl.multiple_of(step * chunk, chunk)
@@ -134,11 +156,10 @@
             lax.broadcasted_iota(jnp.int32, (16, chunk), 0) == 0, flag, 0.0
         ).astype(BF16)
         for side, values, where_to in ((0, right_s, span), (1, left_s, span_b)):
-            jac = facej[side, :, :, span]
             for g in range(fields):
                 total = None
                 for f in range(fields):
-                    entry = jac[g, f : f + 1, :]
+                    entry = facej[g, f, side : side + 1, span]
                     if f == g:
                         entry = entry - visc[g] * flag
                     term = entry * values[f * modes : (f + 1) * modes, :]
@@ -147,6 +168,8 @@
             terms[wide : wide + 16, where_to] = mark
 
     image = matmul(terms[...], hot[...], ((1,), (1,)))
+    for name in names[9:]:
+        fetch(name).wait()
     flagged = image[wide : wide + 1, :]
     rows = []
     for g in range(fields):
@@ -174,10 +197,16 @@
     ).astype(BF16)
     top = lax.broadcasted_iota(jnp.int32, (16, cells), 0) == 0
     gram = None
+
+    def give(g):
+        return pltpu.make_async_copy(
+            stacked.at[g, pl.ds(0, modes)], tb_out.at[g], tb_sem.at[g]
+        )
+
     for g in range(fields):
         basis_g = (rows[g] + arrived[g * modes : (g + 1) * modes]).astype(BF16)
-        tb_out[g] = basis_g
         stacked[g, :modes, :] = basis_g
+        give(g).start()
         shift = jnp.sum(matmul(weights, basis_g, ((1,), (0,))), axis=0, keepdims=True)
         resid = base[g : g + 1, :] + row_scale * shift
         stacked[g, modes : modes + 16, :] = jnp.where(top, resid, 0.0).astype(BF16)
@@ -263,6 +292,9 @@
 
     gram_out[...] = summed[...]
 
+    for g in range(fields):
+        give(g).wait()
+
     for m, (dr, dc) in enumerate(OFFSETS):
         @pl.when(inside_grid(dr, dc))
         def _():
@@ -294,41 +326,68 @@
     def across(x, s):
         return jnp.broadcast_to(x[s : s + 1, :], shape)
 
+    def along(x, c):
+        return jnp.broadcast_to(x[:, c : c + 1], shape)
+
     rows = [gram[t] * (row_scale * row_scale) for t in range(tiles)]
-    done = [jnp.zeros(shape, F32) for _ in range(tiles)]
+    done = []
     for p in range(tiles):
-        columns = range(8 * p, min(8 * p + 8, order))
-        held = {
-            j: [jnp.broadcast_to(rows[t][:, j : j + 1], shape) for t in range(tiles)]
-            for j in columns
+        count = min(8, order - 8 * p)
+        line = [across(rows[p], i) for i in range(count)]
+        entry = {
+            (i, k): along(line[i], 8 * p + k) for i in range(count) for k in range(i, count)
         }
-        for j in columns:
-            s = j % 8
-            here = sub == s
-            inverse = lax.rsqrt(across(held[j][p], s))
-            pivot_row = across(rows[p], s) * inverse
-            done[p] = jnp.where(here, pivot_row, done[p])
-            if j == modes:
-                break
-            scaled = [x * inverse for x in held[j]]
-            for t in range(tiles):
-                new = rows[t] - scaled[t] * pivot_row
-                rows[t] = jnp.where(here, pivot_row * inverse, new) if t == p else new
-            for i in columns:
-                if i <= j:
-                    continue
-                entry = across(scaled[p], i % 8)
-                for t in range(tiles):
-                    new = held[i][t] - scaled[t] * entry
-                    held[i][t] = jnp.where(here, entry * inverse, new) if t == p else new
+        last = p == tiles - 1
+        column = {
+            t: [along(rows[t], 8 * p + j) for j in range(count)]
+            for t in range(tiles) if t != p and not last
+        }
+        ahead = list(column[p + 1]) if not last else []
+        factored, inverse, scaled = [], [], []
+        for j in range(count):
+            root = lax.rsqrt(entry[j, j])
+            inverse.append(root * root)
+            factored.append(line[j] * root)
+            scaled.append(line[j] * inverse[j])
+            for i in range(j + 1, count):
+                ratio = entry[j, i] * inverse[j]
+                for k in range(i, count):
+                    entry[i, k] = entry[i, k] - ratio * entry[j, k]
+                line[i] = line[i] - ratio * line[j]
+                ahead[i] = ahead[i] - ratio * ahead[j]
+        tile = factored[0]
+        for j in range(1, count):
+            tile = jnp.where(sub == j, factored[j], tile)
+        done.append(tile)
+        if last:
+            break
+        new = rows[p + 1]
+        for j in range(count):
+            new = new - ahead[j] * scaled[j]
+        rows[p + 1] = new
+        reduced = list(scaled)
+        for j in range(count - 1, -1, -1):
+            for k in range(j + 1, count):
+                reduced[j] = reduced[j] - entry[j, k] * inverse[j] * reduced[k]
+        for t in range(tiles):
+            if t == p or t == p + 1:
+                continue
+            new = rows[t]
+            for j in range(count):
+                new = new - column[t][j] * reduced[j]
+            rows[t] = new
+        tile = reduced[0]
+        for j in range(1, count):
+            tile = jnp.where(sub == j, reduced[j], tile)
+        rows[p] = tile
     solved = jnp.zeros(shape, F32)
     for t in range(tiles):
         kept = jnp.where(lane >= sub + 8 * t, done[t], 0.0)
         count = min(8, order - 8 * t)
         upper[8 * t : 8 * t + count, :] = kept[:count, :order]
         if 8 * t < modes:
-            last = jnp.broadcast_to(rows[t][:, modes : modes + 1], shape)
-            solved = solved + jnp.where(lane == sub + 8 * t, last, 0.0)
+            tail = along(rows[t], modes)
+            solved = solved + jnp.where(lane == sub + 8 * t, tail, 0.0)
     step[...] = (jnp.sum(solved, axis=0, keepdims=True) * (-1.0 / row_scale))[:, :modes]
     passing.wait()
 
@@ -346,7 +405,7 @@
     tiles = (modes + 1 + 7) // 8
     chunk = 256
     vmem = pl.BlockSpec(memory_space=pltpu.VMEM)
-    smem = pl.BlockSpec(memory_space=pltpu.SMEM)
+    hbm = pl.BlockSpec(memory_space=pltpu.HBM)
     dma = pltpu.SemaphoreType.DMA
     test_basis, gram = pl.pallas_call(
         functools.partial(assemble, nrow, ncol, row_scale, tiles, chunk),
@@ -354,9 +413,23 @@
             jax.ShapeDtypeStruct((fields, modes, cells), BF16),
             jax.ShapeDtypeStruct((tiles, 8, 128), F32),
         ),
-        in_specs=[vmem, vmem, vmem, vmem, vmem, smem, vmem, vmem, smem, vmem, vmem, vmem],
-        out_specs=(vmem, vmem),
+        in_specs=[hbm] * 12,
+        out_specs=(hbm, vmem),
         scratch_shapes=[
+            pltpu.VMEM((fields, modes, cells), BF16),
+            pltpu.VMEM((fields, fields, cells), F32),
+            pltpu.VMEM((2, faces), jnp.int32),
+            pltpu.VMEM((fields, fields, 2, faces), F32),
+            pltpu.VMEM((1, faces), jnp.int32),
+            pltpu.SMEM((fields,), F32),
+            pltpu.VMEM((1, SLOTS), jnp.int32),
+            pltpu.VMEM((fields, fields, SLOTS), F32),
+            pltpu.SMEM((8,), jnp.int32),
+            pltpu.VMEM((1, SLOTS), jnp.int32),
+            pltpu.VMEM((1, modes), F32),
+            pltpu.VMEM((fields, cells), F32),
+            dma((12,)),
+            dma((fields,)),
             pltpu.VMEM((cells, 2 * faces), BF16),
             pltpu.VMEM((wide + 16, 2 * faces), BF16),
             pltpu.VMEM((wide, chunk), F32),
@@ -371,14 +444,15 @@
             dma((8,)), dma((8,)), dma((tiles,)), dma((devices,)), dma((devices,)), dma((tiles,)),
         ],
         compiler_params=pltpu.CompilerParams(
-            collective_id=0, has_side_effects=True, vmem_limit_bytes=48 * 1024 * 1024
+            collective_id=0, has_side_effects=True, vmem_limit_bytes=64 * 1024 * 1024 - 65536
         ),
         cost_estimate=pl.CostEstimate(
             flops=8 * wide * cells * faces, bytes_accessed=3_000_000, transcendentals=0
         ),
         name="assemble",
     )(
-        reduced_basis, cell_jacobian, face_cells, face_jacobian, limiter_flags.reshape(1, -1),
+        reduced_basis, cell_jacobian, face_cells, face_jacobian.transpose(1, 2, 0, 3),
+        limiter_flags.reshape(1, -1),
         viscosity, ghost_cells.reshape(1, -1), ghost_jacobian, ghost_counts,
         receive_cells.reshape(1, -1), coordinates.reshape(1, -1), base_residual,
     )
@@ -389,9 +463,10 @@
             jax.ShapeDtypeStruct((1, modes), F32),
             jax.ShapeDtypeStruct((fields, modes, cells), BF16),
         ),
-        in_specs=[vmem, pl.BlockSpec(memory_space=pl.ANY)],
-        out_specs=(vmem, vmem, pl.BlockSpec(memory_space=pl.ANY)),
+        in_specs=[vmem, hbm],
+        out_specs=(vmem, vmem, hbm),
         scratch_shapes=[pltpu.SemaphoreType.DMA],
+        compiler_params=pltpu.CompilerParams(vmem_limit_bytes=64 * 1024 * 1024 - 65536),
         name="factor",
     )(gram, test_basis)
     return test_basis, upper, step.reshape(modes)

time: 47.3 us -> 42.6 us (0.901)
  local copies, waits for them, and re-layouts: 4.78 us -> 0 us
    unnamed x27 -> x0, local copies, waits for them, and re-layouts: 4.78 us -> none
where the time goes in v2:
time: 42.6 us; the launch traced here: 42.4 us
  Pallas kernels  41.8 us (98%)
  between operations  0.64 us (2%)
    pallas_call x1, Pallas kernels, local(): pl.pallas_call(functools.partial(assemble, nrow, ncol, row_scale, tiles,...  24.4 us
    pallas_call x1, Pallas kernels, local(): pl.pallas_call(functools.partial(factor, modes, row_scale), out_shape=(ja...  17.4 us

profile of v2, /device:TPU:0, one launch (start us, length us, event | category | flops | bytes accessed | tf_op | source)
XLA Modules:
  0.0 42.4 jit_solution(10947334611497796328)
XLA Ops:
  0.6 24.4 %assemble.1 = (bf16[5,96,512]{2,1,0:T(8,128)(2,1)}, f32[13,8,128]{2,1,0:T(8,128)}) custom-call(bf16[5,96,512]{2,1,0:T(8,128)(2,1)} %basis_h.1, f32[5,5,512]{2,1,0:T(8,128)} %cellj_h.1, s32[2,1024]{1,0:T(2,128)} %facec_h.1, f32[5,5,2,1024]{3,2,1,0:T(2,128)} %bitcast.6, s32[1,1024]{1,0:T(1,128)} %bitcast.7, f32[5]{0:T(128)} %visc_h.1, s32[1,160]{1,0:T(1,128)} %bitcast.8, ...), custom_call_target="tpu_custom_call" | custom-call | flops 2013265920 | bytes 3000000 | tf_op jit(solution)/shard_map/assemble/pallas_call | solution.py:410
  25.0 17.4 %factor.1 = (f32[97,97]{1,0:T(8,128)}, f32[1,96]{1,0:T(1,128)}, bf16[5,96,512]{2,1,0:T(8,128)(2,1)}) custom-call(f32[13,8,128]{2,1,0:T(8,128)} %get-tuple-element.8.gram, bf16[5,96,512]{2,1,0:T(8,128)(2,1)} %get-tuple-element.9.tb_in), custom_call_target="tpu_custom_call" | custom-call | tf_op jit(solution)/shard_map/factor/pallas_call | solution.py:459

commit v3 on v2

--- a/solution.py
+++ b/solution.py
@@ -34,7 +34,7 @@
 
 
 def assemble(
-    nrow, ncol, row_scale, tiles, chunk,
+    nrow, ncol, row_scale, last_tile, tiles, chunk,
     basis_h, cellj_h, facec_h, facej_h, flags_h, visc_h, ghostc_h, ghostj_h, counts_h, recvc_h,
     coords_h, base_h,
     tb_out, gram_out,
@@ -69,11 +69,9 @@
 
     barrier = pltpu.get_barrier_semaphore()
 
-    @pl.loop(0, devices)
-    def _(d):
-        @pl.when(d != me)
-        def _():
-            pl.semaphore_signal(barrier, inc=1, device_id=place(d), device_id_type=MESH)
+    others = [lax.rem(me + k, jnp.int32(devices)) for k in range(1, devices)]
+    for d in others:
+        pl.semaphore_signal(barrier, inc=1, device_id=place(d), device_id_type=MESH)
 
     for name in names[:5]:
         fetch(name).wait()
@@ -104,7 +102,6 @@
     target = jnp.where(edge < 0, lane, lane + (edge >> 3) * (EDGE_ROWS - EDGE_CAP))
     spread = jnp.where(sub == target, 1.0, 0.0).astype(BF16)
     sent[...] = matmul(spread, partial, ((1,), (1,))).astype(BF16)
-    placed = matmul(spread, one_hot(recvc[...], cells), ((1,), (1,))).astype(BF16)
 
     def inside_grid(dr, dc):
         ok = (row + dr >= 0) & (row + dr < nrow)
@@ -136,26 +133,29 @@
         def _():
             halo(m).start()
 
+    placed = matmul(spread, one_hot(recvc[...], cells), ((1,), (1,))).astype(BF16)
+
     for name in names[5:9]:
         fetch(name).wait()
 
-    @pl.loop(0, faces // chunk)
-    def _(step):
-        at = pl.multiple_of(step * chunk, chunk)
-        span = pl.ds(at, chunk)
-        span_b = pl.ds(pl.multiple_of(at + faces, chunk), chunk)
+    for number in range(faces // chunk):
+        at = number * chunk
+        span = slice(at, at + chunk)
+        span_b = slice(at + faces, at + faces + chunk)
         pair = facec[:, span]
         hot_a = one_hot(pair[0:1], cells)
         hot_b = one_hot(pair[1:2], cells)
         hot[:, span] = hot_a
         hot[:, span_b] = hot_b
-        left_s[...] = matmul(flat, hot_a, ((1,), (0,)))
-        right_s[...] = matmul(flat, hot_b, ((1,), (0,)))
+        left = left_s.at[number % 2]
+        right = right_s.at[number % 2]
+        left[...] = matmul(flat, hot_a, ((1,), (0,)))
+        right[...] = matmul(flat, hot_b, ((1,), (0,)))
         flag = flags[:, span].astype(F32)
         mark = jnp.where(
             lax.broadcasted_iota(jnp.int32, (16, chunk), 0) == 0, flag, 0.0
         ).astype(BF16)
-        for side, values, where_to in ((0, right_s, span), (1, left_s, span_b)):
+        for side, values, where_to in ((0, right, span), (1, left, span_b)):
             for g in range(fields):
                 total = None
                 for f in range(fields):
@@ -203,33 +203,45 @@
             stacked.at[g, pl.ds(0, modes)], tb_out.at[g], tb_sem.at[g]
         )
 
-    for g in range(fields):
-        basis_g = (rows[g] + arrived[g * modes : (g + 1) * modes]).astype(BF16)
-        stacked[g, :modes, :] = basis_g
-        give(g).start()
-        shift = jnp.sum(matmul(weights, basis_g, ((1,), (0,))), axis=0, keepdims=True)
+    images = [
+        (rows[g] + arrived[g * modes : (g + 1) * modes]).astype(BF16) for g in range(fields)
+    ]
+    for g in range(fields):
+        stacked[g, :modes, :] = images[g]
+    for g in range(fields):
+        shift = jnp.sum(matmul(weights, images[g], ((1,), (0,))), axis=0, keepdims=True)
         resid = base[g : g + 1, :] + row_scale * shift
         stacked[g, modes : modes + 16, :] = jnp.where(top, resid, 0.0).astype(BF16)
         stacked[g, modes + 16 :, :] = jnp.zeros((128 - modes - 16, cells), BF16)
+    for g in range(fields):
         x = stacked[g]
         part = matmul(x, x, ((1,), (1,)))
         gram = part if gram is None else gram + part
-    gram_s[...] = gram[: tiles * 8].reshape(tiles, 8, 128)
+    lane = lax.broadcasted_iota(jnp.int32, (8, 128), 1)
+    for t in range(tiles):
+        low = gram[8 * t : 8 * t + 8]
+        u = last_tile - t
+        if u > t:
+            high = pltpu.roll(gram[8 * u : 8 * u + 8], 8 * (t + 1), 1)
+            keep = (lane >= 8 * t) & (lane < 8 * (last_tile + 1))
+            low = jnp.where(keep, low, high)
+        gram_s[t] = low
 
     def owner(t):
-        return (t * devices) // tiles
-
-    my_tile = lax.div(me * tiles + (devices - 1), jnp.int32(devices))
-    tile = jnp.minimum(my_tile, tiles - 1)
-    owns = (my_tile < tiles) & (lax.div(tile * devices, jnp.int32(tiles)) == me)
+        return (t * nrow) // tiles * ncol + (ncol - 1) // 2 + t % 2
+
+    owns, tile = me == owner(0), jnp.int32(0)
+    for t in range(1, tiles):
+        owns = owns | (me == owner(t))
+        tile = jnp.where(me == owner(t), t, tile)
 
     def up(t):
         o = owner(t)
         return pltpu.make_async_remote_copy(
             src_ref=gram_s.at[t],
             dst_ref=parts.at[me],
-            send_sem=up_send.at[t],
-            recv_sem=up_recv.at[me],
+            send_sem=up_send,
+            recv_sem=up_recv,
             device_id=(jnp.int32(o // ncol), jnp.int32(o % ncol)),
             device_id_type=MESH,
         )
@@ -243,52 +255,41 @@
         def _():
             parts[me] = gram_s[t]
 
-    def down(d):
+    for g in range(fields):
+        give(g).start()
+
+    def many(ref, count, send_sem, recv_sem):
         return pltpu.make_async_remote_copy(
-            src_ref=mine,
-            dst_ref=summed.at[tile],
-            send_sem=down_send.at[d],
-            recv_sem=down_recv.at[tile],
-            device_id=place(d),
+            src_ref=ref.at[pl.ds(0, count)],
+            dst_ref=ref.at[pl.ds(0, count)],
+            send_sem=send_sem,
+            recv_sem=recv_sem,
+            device_id=place(lax.rem(me + 1, jnp.int32(devices))),
             device_id_type=MESH,
         )
 
     @pl.when(owns)
     def _():
-        @pl.loop(0, devices)
-        def _(d):
-            @pl.when(d != me)
-            def _():
-                pltpu.make_async_remote_copy(
-                    src_ref=mine,
-                    dst_ref=parts.at[d],
-                    send_sem=down_send.at[d],
-                    recv_sem=up_recv.at[d],
-                    device_id=place(d),
-                    device_id_type=MESH,
-                ).wait_recv()
-
+        many(parts, devices - 1, down_send, up_recv).wait_recv()
         total = jnp.sum(parts[...], axis=0)
         mine[...] = total
         summed[tile] = total
 
-        @pl.loop(0, devices)
-        def _(d):
-            @pl.when(d != me)
-            def _():
-                down(d).start()
-
-    for t in range(tiles):
-        @pl.when(me != owner(t))
-        def _():
+        for d in others:
             pltpu.make_async_remote_copy(
                 src_ref=mine,
-                dst_ref=summed.at[t],
-                send_sem=up_send.at[t],
-                recv_sem=down_recv.at[t],
-                device_id=place(jnp.int32(owner(t))),
+                dst_ref=summed.at[tile],
+                send_sem=down_send,
+                recv_sem=down_recv,
+                device_id=place(d),
                 device_id_type=MESH,
-            ).wait_recv()
+            ).start()
+
+        many(summed, tiles - 1, up_send, down_recv).wait_recv()
+
+    @pl.when(jnp.logical_not(owns))
+    def _():
+        many(summed, tiles, up_send, down_recv).wait_recv()
 
     gram_out[...] = summed[...]
 
@@ -300,25 +301,22 @@
         def _():
             halo(m).wait_send()
 
-    for t in range(tiles):
-        @pl.when(me != owner(t))
-        def _():
-            up(t).wait_send()
-
     @pl.when(owns)
     def _():
-        @pl.loop(0, devices)
-        def _(d):
-            @pl.when(d != me)
-            def _():
-                down(d).wait_send()
-
-
-def factor(modes, row_scale, gram, tb_in, upper, step, tb_out, sem):
-    passing = pltpu.make_async_copy(tb_in, tb_out, sem)
-    passing.start()
-    tiles = gram.shape[0]
+        many(gram_s, tiles - 1, up_send, up_recv).wait_send()
+        many(parts, devices - 1, down_send, up_recv).wait_send()
+
+    @pl.when(jnp.logical_not(owns))
+    def _():
+        many(gram_s, tiles, up_send, up_recv).wait_send()
+
+
+def factor(modes, row_scale, gram, tb_in, upper, step, tb_out, held, sem):
+    coming = pltpu.make_async_copy(tb_in, held, sem.at[0])
+    going = pltpu.make_async_copy(held, tb_out, sem.at[1])
+    coming.start()
     order = modes + 1
+    tiles = (order + 7) // 8
     shape = (8, 128)
     sub = lax.broadcasted_iota(jnp.int32, shape, 0)
     lane = lax.broadcasted_iota(jnp.int32, shape, 1)
@@ -329,7 +327,19 @@
     def along(x, c):
         return jnp.broadcast_to(x[:, c : c + 1], shape)
 
-    rows = [gram[t] * (row_scale * row_scale) for t in range(tiles)]
+    half = []
+    for t in range(tiles):
+        u = tiles - 1 - t
+        if t <= u:
+            tile = gram[t]
+        else:
+            tile = pltpu.roll(gram[u], 128 - 8 * (u + 1), 1)
+        half.append(jnp.where(lane >= sub + 8 * t, tile * (row_scale * row_scale), 0.0))
+    full = jnp.concatenate(half + [jnp.zeros(shape, F32)] * (16 - tiles), axis=0)
+    mirror = full.T
+    rows = [
+        jnp.where(lane >= sub + 8 * t, half[t], mirror[8 * t : 8 * t + 8]) for t in range(tiles)
+    ]
     done = []
     for p in range(tiles):
         count = min(8, order - 8 * p)
@@ -361,6 +371,9 @@
         done.append(tile)
         if last:
             break
+        if p == 3:
+            coming.wait()
+            going.start()
         new = rows[p + 1]
         for j in range(count):
             new = new - ahead[j] * scaled[j]
@@ -389,7 +402,7 @@
             tail = along(rows[t], modes)
             solved = solved + jnp.where(lane == sub + 8 * t, tail, 0.0)
     step[...] = (jnp.sum(solved, axis=0, keepdims=True) * (-1.0 / row_scale))[:, :modes]
-    passing.wait()
+    going.wait()
 
 
 def local(
@@ -402,13 +415,14 @@
     devices = nrow * ncol
     wide = fields * modes
     row_scale = float((fields * cells * devices) ** (-0.5))
-    tiles = (modes + 1 + 7) // 8
+    blocks = (modes + 1 + 7) // 8
+    tiles = (blocks + 1) // 2
     chunk = 256
     vmem = pl.BlockSpec(memory_space=pltpu.VMEM)
     hbm = pl.BlockSpec(memory_space=pltpu.HBM)
     dma = pltpu.SemaphoreType.DMA
     test_basis, gram = pl.pallas_call(
-        functools.partial(assemble, nrow, ncol, row_scale, tiles, chunk),
+        functools.partial(assemble, nrow, ncol, row_scale, blocks - 1, tiles, chunk),
         out_shape=(
             jax.ShapeDtypeStruct((fields, modes, cells), BF16),
             jax.ShapeDtypeStruct((tiles, 8, 128), F32),
@@ -432,8 +446,8 @@
             dma((fields,)),
             pltpu.VMEM((cells, 2 * faces), BF16),
             pltpu.VMEM((wide + 16, 2 * faces), BF16),
-            pltpu.VMEM((wide, chunk), F32),
-            pltpu.VMEM((wide, chunk), F32),
+            pltpu.VMEM((2, wide, chunk), F32),
+            pltpu.VMEM((2, wide, chunk), F32),
             pltpu.VMEM((SENT_ROWS, wide), BF16),
             pltpu.VMEM((SENT_ROWS, wide), BF16),
             pltpu.VMEM((fields, 128, cells), BF16),
@@ -441,7 +455,7 @@
             pltpu.VMEM((devices, 8, 128), F32),
             pltpu.VMEM((8, 128), F32),
             pltpu.VMEM((tiles, 8, 128), F32),
-            dma((8,)), dma((8,)), dma((tiles,)), dma((devices,)), dma((devices,)), dma((tiles,)),
+            dma((8,)), dma((8,)), dma, dma, dma, dma,
         ],
         compiler_params=pltpu.CompilerParams(
             collective_id=0, has_side_effects=True, vmem_limit_bytes=64 * 1024 * 1024 - 65536
@@ -465,7 +479,7 @@
         ),
         in_specs=[vmem, hbm],
         out_specs=(vmem, vmem, hbm),
-        scratch_shapes=[pltpu.SemaphoreType.DMA],
+        scratch_shapes=[pltpu.VMEM((fields, modes, cells), BF16), dma((2,))],
         compiler_params=pltpu.CompilerParams(vmem_limit_bytes=64 * 1024 * 1024 - 65536),
         name="factor",
     )(gram, test_basis)

time: 42.6 us -> 26.6 us (0.62)
  Pallas kernels: 41.8 us -> 25.7 us
    pallas_call x1, Pallas kernels: 17.4 us -> 5.47 us  [local(): pl.pallas_call(functools.partial(factor, modes, row_scale), out_shape=(ja...]
    pallas_call x1, Pallas kernels: 24.4 us -> 20.2 us  [local(): pl.pallas_call(functools.partial(assemble, nrow, ncol, row_scale, blocks...]
where the time goes in v3:
time: 26.6 us; the launch traced here: 26.3 us
  Pallas kernels  25.7 us (97%)
  between operations  0.64 us (2%)
    pallas_call x1, Pallas kernels, local(): pl.pallas_call(functools.partial(assemble, nrow, ncol, row_scale, blocks...  20.2 us
    pallas_call x1, Pallas kernels, local(): pl.pallas_call(functools.partial(factor, modes, row_scale), out_shape=(ja...  5.47 us

profile of v3, /device:TPU:0, one launch (start us, length us, event | category | flops | bytes accessed | tf_op | source)
XLA Modules:
  0.0 26.3 jit_solution(18364148807014041246)
XLA Ops:
  0.6 20.2 %assemble.1 = (bf16[5,96,512]{2,1,0:T(8,128)(2,1)}, f32[7,8,128]{2,1,0:T(8,128)}) custom-call(bf16[5,96,512]{2,1,0:T(8,128)(2,1)} %basis_h.1, f32[5,5,512]{2,1,0:T(8,128)} %cellj_h.1, s32[2,1024]{1,0:T(2,128)} %facec_h.1, f32[5,5,2,1024]{3,2,1,0:T(2,128)} %bitcast.6, s32[1,1024]{1,0:T(1,128)} %bitcast.7, f32[5]{0:T(128)} %visc_h.1, s32[1,160]{1,0:T(1,128)} %bitcast.8, ...), custom_call_target="tpu_custom_call" | custom-call | flops 2013265920 | bytes 3000000 | tf_op jit(solution)/shard_map/assemble/pallas_call | solution.py:424
  20.8 5.5 %factor.1 = (f32[97,97]{1,0:T(8,128)}, f32[1,96]{1,0:T(1,128)}, bf16[5,96,512]{2,1,0:T(8,128)(2,1)}) custom-call(f32[7,8,128]{2,1,0:T(8,128)} %get-tuple-element.8.gram, bf16[5,96,512]{2,1,0:T(8,128)(2,1)} %get-tuple-element.9.tb_in), custom_call_target="tpu_custom_call" | custom-call | tf_op jit(solution)/shard_map/factor/pallas_call | solution.py:473

commit v4 on v3

--- a/solution.py
+++ b/solution.py
@@ -138,14 +138,26 @@
     for name in names[5:9]:
         fetch(name).wait()
 
+    for name in names[9:]:
+        fetch(name).wait()
+    own = []
+    for g in range(fields):
+        total = None
+        for f in range(fields):
+            term = cellj[g, f : f + 1, :] * basis[f].astype(F32)
+            total = term if total is None else total + term
+        own.append(total)
+
+    image, first = None, 0
     for number in range(faces // chunk):
         at = number * chunk
         span = slice(at, at + chunk)
-        span_b = slice(at + faces, at + faces + chunk)
+        span_a = slice(2 * at, 2 * at + chunk)
+        span_b = slice(2 * at + chunk, 2 * at + 2 * chunk)
         pair = facec[:, span]
         hot_a = one_hot(pair[0:1], cells)
         hot_b = one_hot(pair[1:2], cells)
-        hot[:, span] = hot_a
+        hot[:, span_a] = hot_a
         hot[:, span_b] = hot_b
         left = left_s.at[number % 2]
         right = right_s.at[number % 2]
@@ -155,7 +167,7 @@
         mark = jnp.where(
             lax.broadcasted_iota(jnp.int32, (16, chunk), 0) == 0, flag, 0.0
         ).astype(BF16)
-        for side, values, where_to in ((0, right, span), (1, left, span_b)):
+        for side, values, where_to in ((0, right, span_a), (1, left, span_b)):
             for g in range(fields):
                 total = None
                 for f in range(fields):
@@ -167,19 +179,17 @@
                 terms[g * modes : (g + 1) * modes, where_to] = total.astype(BF16)
             terms[wide : wide + 16, where_to] = mark
 
-    image = matmul(terms[...], hot[...], ((1,), (1,)))
-    for name in names[9:]:
-        fetch(name).wait()
+        if 2 * (number + 1) == faces // chunk or number + 1 == faces // chunk:
+            ready = slice(first, 2 * at + 2 * chunk)
+            first = ready.stop
+            part = matmul(terms[:, ready], hot[:, ready], ((1,), (1,)))
+            image = part if image is None else image + part
+
     flagged = image[wide : wide + 1, :]
     rows = []
     for g in range(fields):
-        total = image[g * modes : (g + 1) * modes, :]
-        for f in range(fields):
-            entry = cellj[g, f : f + 1, :]
-            if f == g:
-                entry = entry + visc[g] * flagged
-            total = total + entry * basis[f].astype(F32)
-        rows.append(total)
+        total = own[g] + image[g * modes : (g + 1) * modes, :]
+        rows.append(total + (visc[g] * flagged) * basis[g].astype(F32))
 
     for m, (dr, dc) in enumerate(OFFSETS):
         @pl.when(inside_grid(-dr, -dc))
@@ -362,7 +372,7 @@
             for i in range(j + 1, count):
                 ratio = entry[j, i] * inverse[j]
                 for k in range(i, count):
-                    entry[i, k] = entry[i, k] - ratio * entry[j, k]
+                    entry[i, k] = entry[i, k] - (entry[j, i] * entry[j, k]) * inverse[j]
                 line[i] = line[i] - ratio * line[j]
                 ahead[i] = ahead[i] - ratio * ahead[j]
         tile = factored[0]

time: 26.6 us -> 26.8 us (level)
  no operation moved by 1% of the time
where the time goes in v4:
time: 26.8 us; the launch traced here: 26.5 us
  Pallas kernels  25.9 us (97%)
  between operations  0.64 us (2%)
    pallas_call x1, Pallas kernels, local(): pl.pallas_call(functools.partial(assemble, nrow, ncol, row_scale, blocks...  20.4 us
    pallas_call x1, Pallas kernels, local(): pl.pallas_call(functools.partial(factor, modes, row_scale), out_shape=(ja...  5.47 us

profile of v4, /device:TPU:0, one launch (start us, length us, event | category | flops | bytes accessed | tf_op | source)
XLA Modules:
  0.0 26.5 jit_solution(5666567273583367531)
XLA Ops:
  0.6 20.4 %assemble.1 = (bf16[5,96,512]{2,1,0:T(8,128)(2,1)}, f32[7,8,128]{2,1,0:T(8,128)}) custom-call(bf16[5,96,512]{2,1,0:T(8,128)(2,1)} %basis_h.1, f32[5,5,512]{2,1,0:T(8,128)} %cellj_h.1, s32[2,1024]{1,0:T(2,128)} %facec_h.1, f32[5,5,2,1024]{3,2,1,0:T(2,128)} %bitcast.6, s32[1,1024]{1,0:T(1,128)} %bitcast.7, f32[5]{0:T(128)} %visc_h.1, s32[1,160]{1,0:T(1,128)} %bitcast.8, ...), custom_call_target="tpu_custom_call" | custom-call | flops 2013265920 | bytes 3000000 | tf_op jit(solution)/shard_map/assemble/pallas_call | solution.py:434
  21.0 5.5 %factor.1 = (f32[97,97]{1,0:T(8,128)}, f32[1,96]{1,0:T(1,128)}, bf16[5,96,512]{2,1,0:T(8,128)(2,1)}) custom-call(f32[7,8,128]{2,1,0:T(8,128)} %get-tuple-element.8.gram, bf16[5,96,512]{2,1,0:T(8,128)(2,1)} %get-tuple-element.9.tb_in), custom_call_target="tpu_custom_call" | custom-call | tf_op jit(solution)/shard_map/factor/pallas_call | solution.py:483

commit v5 on v3

--- a/solution.py
+++ b/solution.py
@@ -52,7 +52,7 @@
     def place(d):
         return (lax.div(d, jnp.int32(ncol)), lax.rem(d, jnp.int32(ncol)))
 
-    names = ("basis", "ghostc", "counts", "ghostj", "recvc", "facec", "flags", "visc", "facej",
+    names = ("facec", "ghostc", "basis", "counts", "ghostj", "recvc", "flags", "visc", "facej",
              "cellj", "coords", "base")
     inputs = dict(
         basis=(basis_h, basis), ghostc=(ghostc_h, ghostc), counts=(counts_h, counts),
@@ -73,7 +73,13 @@
     for d in others:
         pl.semaphore_signal(barrier, inc=1, device_id=place(d), device_id_type=MESH)
 
-    for name in names[:5]:
+    fetch(names[0]).wait()
+    for at in range(0, faces, chunk):
+        for side in range(2):
+            pair = facec[side : side + 1, at : at + chunk]
+            hot[:, side * faces + at : side * faces + at + chunk] = one_hot(pair, cells)
+
+    for name in names[1:6]:
         fetch(name).wait()
     flat = basis[...].reshape(wide, cells)
 
@@ -135,22 +141,17 @@
 
     placed = matmul(spread, one_hot(recvc[...], cells), ((1,), (1,))).astype(BF16)
 
-    for name in names[5:9]:
+    for name in names[6:9]:
         fetch(name).wait()
 
     for number in range(faces // chunk):
         at = number * chunk
         span = slice(at, at + chunk)
         span_b = slice(at + faces, at + faces + chunk)
-        pair = facec[:, span]
-        hot_a = one_hot(pair[0:1], cells)
-        hot_b = one_hot(pair[1:2], cells)
-        hot[:, span] = hot_a
-        hot[:, span_b] = hot_b
         left = left_s.at[number % 2]
         right = right_s.at[number % 2]
-        left[...] = matmul(flat, hot_a, ((1,), (0,)))
-        right[...] = matmul(flat, hot_b, ((1,), (0,)))
+        left[...] = matmul(flat, hot[:, span], ((1,), (0,)))
+        right[...] = matmul(flat, hot[:, span_b], ((1,), (0,)))
         flag = flags[:, span].astype(F32)
         mark = jnp.where(
             lax.broadcasted_iota(jnp.int32, (16, chunk), 0) == 0, flag, 0.0
@@ -344,8 +345,9 @@
     for p in range(tiles):
         count = min(8, order - 8 * p)
         line = [across(rows[p], i) for i in range(count)]
+        spread = [along(rows[p], 8 * p + k) for k in range(count)]
         entry = {
-            (i, k): along(line[i], 8 * p + k) for i in range(count) for k in range(i, count)
+            (i, k): across(spread[k], i) for i in range(count) for k in range(i, count)
         }
         last = p == tiles - 1
         column = {

time: 26.6 us -> 26.2 us (0.985)
  Pallas kernels: 25.7 us -> 25.3 us
    pallas_call x1, Pallas kernels: 20.2 us -> 19.8 us  [local(): pl.pallas_call(functools.partial(assemble, nrow, ncol, row_scale, blocks...]
where the time goes in v5:
time: 26.2 us; the launch traced here: 25.9 us
  Pallas kernels  25.3 us (97%)
  between operations  0.64 us (2%)
    pallas_call x1, Pallas kernels, local(): pl.pallas_call(functools.partial(assemble, nrow, ncol, row_scale, blocks...  19.8 us
    pallas_call x1, Pallas kernels, local(): pl.pallas_call(functools.partial(factor, modes, row_scale), out_shape=(ja...  5.47 us

profile of v5, /device:TPU:0, one launch (start us, length us, event | category | flops | bytes accessed | tf_op | source)
XLA Modules:
  0.0 25.9 jit_solution(2231269977922097455)
XLA Ops:
  0.6 19.8 %assemble.1 = (bf16[5,96,512]{2,1,0:T(8,128)(2,1)}, f32[7,8,128]{2,1,0:T(8,128)}) custom-call(bf16[5,96,512]{2,1,0:T(8,128)(2,1)} %basis_h.1, f32[5,5,512]{2,1,0:T(8,128)} %cellj_h.1, s32[2,1024]{1,0:T(2,128)} %facec_h.1, f32[5,5,2,1024]{3,2,1,0:T(2,128)} %bitcast.6, s32[1,1024]{1,0:T(1,128)} %bitcast.7, f32[5]{0:T(128)} %visc_h.1, s32[1,160]{1,0:T(1,128)} %bitcast.8, ...), custom_call_target="tpu_custom_call" | custom-call | flops 2013265920 | bytes 3000000 | tf_op jit(solution)/shard_map/assemble/pallas_call | solution.py:426
  20.4 5.5 %factor.1 = (f32[97,97]{1,0:T(8,128)}, f32[1,96]{1,0:T(1,128)}, bf16[5,96,512]{2,1,0:T(8,128)(2,1)}) custom-call(f32[7,8,128]{2,1,0:T(8,128)} %get-tuple-element.8.gram, bf16[5,96,512]{2,1,0:T(8,128)(2,1)} %get-tuple-element.9.tb_in), custom_call_target="tpu_custom_call" | custom-call | tf_op jit(solution)/shard_map/factor/pallas_call | solution.py:475
